TPU v7x, 32 devices: a whole 2x2x4 slice. The times are simulated.
32 devices in a mesh: groups: 2 (over y), section: 4 (over z), dp: 2 (over x), sub: 2 (over core).
Axes of the slice: x: 2, y: 2, z: 4, core: 2. Of those that a mesh axis runs over, the one named last changes fastest.
Arguments:
- inputs: bfloat16 [16, 128, 4096], P(('groups', 'section', 'dp'), None, 'sub'), parts along dimension 0, may hold values from -6 to 6
- queries: bfloat16 [16, 128, 4096], P(('groups', 'section', 'dp'), None, 'sub'), parts along dimension 0, may hold values from -210 to 210
- out_grad: bfloat16 [16, 128, 4096], P(('groups', 'section', 'dp'), None, 'sub'), parts along dimension 0, may hold values from -6 to 6
- lengths: int32 [16], P(('groups', 'section', 'dp')), parts along dimension 0, may hold values from 32 to 128, as said below
- key_matrix: bfloat16 [4096, 512], P('section', 'sub'), may hold values from -0.09375 to 0.09375
- value_matrix: bfloat16 [4096, 512], P('section', 'sub'), may hold values from -0.09375 to 0.09375
Outputs:
- query_grad: bfloat16 [16, 128, 4096], P(('groups', 'section', 'dp'), None, 'sub'), parts along dimension 0
- input_grad: bfloat16 [16, 128, 4096], P(('groups', 'section', 'dp'), None, 'sub'), parts along dimension 0
- key_weight_grad: float32 [8192, 512], P(('groups', 'section'), 'sub'), parts along dimension 0
- value_weight_grad: float32 [8192, 512], P(('groups', 'section'), 'sub'), parts along dimension 0
There are 2 independent parts, one for each index of `groups`. A program takes and returns all parts, laid end to end along the dimension named above; an argument that names none is the same for every part. Nothing has to cross between parts.
Inputs may be any that keep to these rules, and one draw needn't show every extreme that they name: `lengths`: keys at or past a micro-batch's length are excluded; some micro-batch has all 128 tokens valid.
All inputs are finite; a program needn't handle non-finite values.
Results may differ from a plain program's by a relative error of at most 0.011.
The roundings to bfloat16 on the way count: a program that leaves them out, or rounds other values in their place, can miss the bound.
Values may be sent and summed in bfloat16 or wider, within the bound.
A program may use at most 64 MiB of HBM per device.

v0:
```python
import math

import jax
import jax.numpy as jnp
from jax import lax
from jax.sharding import PartitionSpec as P

HEAD_SIZE = 128
QUERY_GROUP = 8


def from_behind(x, axis, by):
    peers = lax.axis_size(axis)
    return lax.ppermute(x, axis, [(i, (i + by) % peers) for i in range(peers)])


def rotary_tables(positions_total, head_width):
    positions = jnp.arange(positions_total, dtype=jnp.float32)[:, None]
    frequency = jnp.exp(
        jnp.arange(head_width // 2, dtype=jnp.float32) * (-2.0 * math.log(10000.0) / head_width)
    )
    angles = positions * frequency[None, :]
    return (jnp.cos(angles)[:, None, :], jnp.sin(angles)[:, None, :])


def apply_rotary(tensor, cosine_table, sine_values_table):
    half_width = tensor.shape[-1] // 2
    leading = tensor[..., :half_width]
    trailing = tensor[..., half_width:]
    return jnp.concatenate(
        [
            leading * cosine_table - trailing * sine_values_table,
            trailing * cosine_table + leading * sine_values_table,
        ],
        axis=-1,
    )


def unrotate(tensor, cosine_table, sine_values_table):
    half_width = tensor.shape[-1] // 2
    leading = tensor[..., :half_width]
    trailing = tensor[..., half_width:]
    return jnp.concatenate(
        [
            leading * cosine_table + trailing * sine_values_table,
            trailing * cosine_table - leading * sine_values_table,
        ],
        axis=-1,
    )


def section_loop(block_term, heading):
    cycle_size = lax.axis_size("section")
    position = lax.axis_index("section")
    opening = block_term(jnp.remainder(position - heading, cycle_size))

    def advance(step_index, carried):
        arrived = from_behind(carried, "section", heading)
        return arrived + block_term(
            jnp.remainder(position - heading * (step_index + 1), cycle_size)
        )

    return lax.fori_loop(1, cycle_size, advance, opening)


def shards(inputs, queries, out_grad, lengths, key_matrix, value_matrix):
    gathered = lax.all_gather(inputs, "sub", axis=2, tiled=True)
    token_rows = gathered[0]
    query_matrix_rows = queries[0]
    gradient_rows = out_grad[0]
    valid_length = lengths[0]
    token_count = token_rows.shape[0]
    local_cols = key_matrix.shape[1]
    kv_local = local_cols // HEAD_SIZE
    score_scale = HEAD_SIZE ** (-0.5)
    joined = jnp.concatenate([key_matrix, value_matrix], axis=1)
    columns = token_rows
    projected = jnp.dot(
        columns,
        lax.all_gather(joined, "section", axis=0, tiled=True),
        preferred_element_type=jnp.float32,
    )
    cosine_table, sine_values_table = rotary_tables(token_count, HEAD_SIZE)
    linear_key = projected[:, :local_cols].reshape(token_count, kv_local, HEAD_SIZE)
    heads_of_value = (
        projected[:, local_cols:].astype(jnp.bfloat16).reshape(token_count, kv_local, HEAD_SIZE)
    )
    rotary_output = apply_rotary(linear_key, cosine_table, sine_values_table).astype(jnp.bfloat16)
    grouped_query = query_matrix_rows.reshape(token_count, kv_local, QUERY_GROUP, HEAD_SIZE)
    grouped_gradient = gradient_rows.reshape(token_count, kv_local, QUERY_GROUP, HEAD_SIZE)
    scores = (
        jnp.einsum(
            "tkgd,ukd->kgtu", grouped_query, rotary_output, preferred_element_type=jnp.float32
        )
        * score_scale
    )
    row_ids = jnp.arange(token_count, dtype=jnp.int32)[:, None]
    col_ids = jnp.arange(token_count, dtype=jnp.int32)[None, :]
    allowed = (col_ids <= row_ids) & (col_ids < valid_length)
    scores = jnp.where(allowed, scores, -1e30)
    row_peak = jnp.max(scores, axis=-1, keepdims=True)
    exponent = jnp.exp(scores - row_peak)
    soft_weights = exponent / jnp.sum(exponent, axis=-1, keepdims=True)
    soft_rounded = soft_weights.astype(jnp.bfloat16)
    prob_grad = jnp.einsum(
        "tkgd,ukd->kgtu", grouped_gradient, heads_of_value, preferred_element_type=jnp.float32
    )
    centre = jnp.sum(soft_weights * prob_grad, axis=-1, keepdims=True)
    logit_grad = (soft_weights * (prob_grad - centre) * score_scale).astype(jnp.bfloat16)
    query_grad = jnp.einsum(
        "kgtu,ukd->tkgd", logit_grad, rotary_output, preferred_element_type=jnp.float32
    )
    query_grad = query_grad.astype(jnp.bfloat16).reshape(
        token_count, kv_local * QUERY_GROUP * HEAD_SIZE
    )
    key_grad_rotated = jnp.einsum(
        "kgtu,tkgd->ukd", logit_grad, grouped_query, preferred_element_type=jnp.float32
    )
    value_grad = jnp.einsum(
        "kgtu,tkgd->ukd", soft_rounded, grouped_gradient, preferred_element_type=jnp.float32
    )
    key_grad = unrotate(key_grad_rotated, cosine_table, sine_values_table)
    proj_grads = jnp.concatenate(
        [key_grad.reshape(token_count, local_cols), value_grad.reshape(token_count, local_cols)],
        axis=1,
    ).astype(jnp.bfloat16)
    partial_grad = lax.dot_general(
        proj_grads,
        lax.all_gather(joined, "section", axis=0, tiled=True),
        (((1,), (1,)), ((), ())),
        preferred_element_type=jnp.float32,
    )
    input_grad = lax.psum_scatter(
        partial_grad[None], "sub", scatter_dimension=2, tiled=True
    ).astype(jnp.bfloat16)
    block_rows = joined.shape[0]
    heading = 1
    scale_down = 1.0 / (lax.axis_size("section") * lax.axis_size("dp"))

    def full_term(block_index):
        columns = lax.dynamic_slice_in_dim(token_rows, block_index * block_rows, block_rows, 1)
        return lax.dot_general(
            columns, proj_grads, (((0,), (0,)), ((), ())), preferred_element_type=jnp.float32
        )

    summed = section_loop(full_term, heading)
    totals = lax.psum(summed, "dp") * scale_down
    return (query_grad[None], input_grad, totals[:, :local_cols], totals[:, local_cols:])


def solution(mesh):
    return jax.shard_map(
        shards,
        mesh=mesh,
        in_specs=(
            P(("groups", "section", "dp"), None, "sub"),
            P(("groups", "section", "dp"), None, "sub"),
            P(("groups", "section", "dp"), None, "sub"),
            P(("groups", "section", "dp")),
            P("section", "sub"),
            P("section", "sub"),
        ),
        out_specs=(
            P(("groups", "section", "dp"), None, "sub"),
            P(("groups", "section", "dp"), None, "sub"),
            P(("groups", "section"), "sub"),
            P(("groups", "section"), "sub"),
        ),
        check_vma=False,
    )
```

profile of v0, /device:TPU:0, one launch (start us, length us, event | category | flops | bytes accessed | tf_op | source)
XLA Modules:
  0.0 349.0 jit_solution(14507134998948112195)
XLA Ops:
  7.2 0.7 all-gather.5.cloned.1.call-update
  8.0 2.3 pad_maximum_fusion
  12.0 9.4 %all-gather.5.cloned.1.call-done = bf16[1,128,4096]{2,1,0:T(8,128)(2,1)} async-done(((bf16[1,128,2048]{2,1,0:T(8,128)(2,1)}), bf16[1,128,4096]{2,1,0:T(8,128)(2,1)}) %all-gather.5.cloned.1.call-update) | async-done | bytes 1048592 | tf_op jit(solution)/shard_map/all_gather | solution.py:67
  21.3 84.1 %all-gather.3.cloned.1.call-done = bf16[4096,512]{1,0:T(8,128)(2,1)} async-done(((bf16[1024,512]{1,0:T(8,128)(2,1)}), bf16[4096,512]{1,0:T(8,128)(2,1)}) %all-gather.3.cloned.1.call-update) | async-done | bytes 4194320 | tf_op jit(solution)/shard_map/all_gather | solution.py:80
  105.4 3.8 %convolution_bitcast_fusion.2 = f32[128,512]{0,1:T(8,128)S(1)} fusion(bf16[4096,512]{1,0:T(8,128)(2,1)} %all-gather.3.cloned.1.call-done, bf16[1,128,4096]{2,1,0:T(8,128)(2,1)} %all-gather.5.cloned.1.call-done), kind=kOutput, calls=%fused_computation.17 | convolution fusion | flops 536870912 | bytes 5505024 | tf_op jit(solution)/shard_map/dot_general | solution.py:78
  109.9 1.5 fusion.38
  111.3 0.7 fusion.12
  112.1 2.1 convolution_bitcast_fusion.4
  114.7 1.8 fusion.21
  116.5 150.9 %while.17 = (s32[]{:T(128)}, f32[1024,512]{1,0:T(8,128)}, s32[]{:T(128)}, bf16[128,4096]{1,0:T(8,128)(2,1)S(1)}, bf16[128,512]{1,0:T(8,128)(2,1)S(1)}, /*index=5...) while((s32[]{:T(128)}, f32[1024,512]{1,0:T(8,128)}, ...), condition=%wide.region_5.6_spmd, body=%wide.region_4.5_spmd.sunk | while | flops 134742032 | bytes 12976468 | solution.py:63
  116.5 49.4 %collective-permute-done = f32[1024,512]{1,0:T(8,128)S(1)} collective-permute-done((f32[1024,512]{1,0:T(8,128)}, f32[1024,512]{1,0:T(8,128)S(1)}, u32[]{:S(2)}, u32[]{:S(2)}) %collective-permute-start) | collective-permute-done | bytes 2097184 | tf_op jit(solution)/shard_map/while/body/eval_jaxpr/ppermute | solution.py:14
  165.9 1.8 convolution_add_fusion.2
  167.7 48.5 %collective-permute-done = f32[1024,512]{1,0:T(8,128)S(1)} collective-permute-done((f32[1024,512]{1,0:T(8,128)}, f32[1024,512]{1,0:T(8,128)S(1)}, u32[]{:S(2)}, u32[]{:S(2)}) %collective-permute-start) | collective-permute-done | bytes 2097184 | tf_op jit(solution)/shard_map/while/body/eval_jaxpr/ppermute | solution.py:14
  216.2 1.8 convolution_add_fusion.2
  218.0 47.6 %collective-permute-done = f32[1024,512]{1,0:T(8,128)S(1)} collective-permute-done((f32[1024,512]{1,0:T(8,128)}, f32[1024,512]{1,0:T(8,128)S(1)}, u32[]{:S(2)}, u32[]{:S(2)}) %collective-permute-start) | collective-permute-done | bytes 2097184 | tf_op jit(solution)/shard_map/while/body/eval_jaxpr/ppermute | solution.py:14
  265.6 1.8 convolution_add_fusion.2
  267.5 5.0 %convolution_bitcast_fusion = f32[1,128,4096]{2,1,0:T(8,128)} fusion(bf16[4096,512]{1,0:T(8,128)(2,1)} %all-gather.3.cloned.1.call-done, bf16[128,256]{0,1:T(8,128)(2,1)S(1)} %bitcast.88, bf16[128,256]{0,1:T(8,128)(2,1)S(1)} %bitcast.85), kind=kOutput, calls=%fused_computation.5 | convolution fusion | flops 537133056 | bytes 6422528 | tf_op jit(solution)/shard_map/dot_general | solution.py:127
  272.6 2.9 convolution_convert_fusion
  275.4 1.0 copy.38
  276.5 52.1 %all-reduce.2.cloned.1.call-done = f32[1024,512]{1,0:T(8,128)} async-done(((f32[1024,512]{1,0:T(8,128)}), f32[1024,512]{1,0:T(8,128)}) %all-reduce.2.cloned.1.call-update) | async-done | bytes 2097168 | tf_op jit(solution)/shard_map/psum | solution.py:147
  328.6 1.8 broadcast_multiply_fusion
  330.4 1.5 fusion.36
  331.9 8.6 %reduce-scatter.2.cloned.1.call-done = f32[1,128,2048]{2,1,0:T(8,128)} async-done(((f32[1,128,4096]{2,1,0:T(8,128)}), f32[1,128,2048]{2,1,0:T(8,128)}) %reduce-scatter.2.cloned.1.call-update) | async-done | bytes 1048592 | tf_op jit(solution)/shard_map/reduce_scatter | solution.py:133
  340.4 2.1 convert_element_type.22
  (36 shorter events, 2.2 us)
Async XLA Ops:
  7.2 3.8 %copy-start.2 = (bf16[1,128,2048]{2,1,0:T(8,128)(2,1)S(1)}, bf16[1,128,2048]{2,1,0:T(8,128)(2,1)}, u32[]{:S(2)}) copy-start(bf16[1,128,2048]{2,1,0:T(8,128)(2,1)} %param.9) | copy-start | bytes 1572868
  7.2 14.1 %all-gather.5.cloned.1.call-start = ((), (), s32[]{:S(2)}) async-start(), calls=%async_computation.2 | async-start | bytes 1572864 | tf_op jit(solution)/shard_map/all_gather | solution.py:67
  7.9 3.4 copy-start.3
  7.9 97.5 %all-gather.3.cloned.1.call-start = ((), (), s32[]{:S(2)}) async-start(), calls=%async_computation.1 | async-start | bytes 5242880 | tf_op jit(solution)/shard_map/all_gather | solution.py:80
  10.3 318.3 %all-reduce.2.cloned.1.call-start = ((), (), s32[]{:S(2)}) async-start(), calls=%async_computation.4 | async-start | bytes 4194304 | tf_op jit(solution)/shard_map/psum | solution.py:147
  109.8 2.3 copy-start.1
  112.1 2.6 copy-start
  116.5 49.4 %collective-permute-start = (f32[1024,512]{1,0:T(8,128)}, f32[1024,512]{1,0:T(8,128)S(1)}, u32[]{:S(2)}, u32[]{:S(2)}) collective-permute-start(f32[1024,512]{1,0:T(8,128)} %get-tuple-element.255), channel_id=1, source_target_pairs={{0,4},{4,8},{8,12},{12,0},{1,5},{5,9},{9,13},{13,1},{2,6},{6,10},{... | collective-permute-start | bytes 6291464 | tf_op jit(solution)/shard_map/while/body/eval_jaxpr/ppermute | solution.py:14
  167.7 48.5 %collective-permute-start = (f32[1024,512]{1,0:T(8,128)}, f32[1024,512]{1,0:T(8,128)S(1)}, u32[]{:S(2)}, u32[]{:S(2)}) collective-permute-start(f32[1024,512]{1,0:T(8,128)} %get-tuple-element.255), channel_id=1, source_target_pairs={{0,4},{4,8},{8,12},{12,0},{1,5},{5,9},{9,13},{13,1},{2,6},{6,10},{... | collective-permute-start | bytes 6291464 | tf_op jit(solution)/shard_map/while/body/eval_jaxpr/ppermute | solution.py:14
  218.0 47.6 %collective-permute-start = (f32[1024,512]{1,0:T(8,128)}, f32[1024,512]{1,0:T(8,128)S(1)}, u32[]{:S(2)}, u32[]{:S(2)}) collective-permute-start(f32[1024,512]{1,0:T(8,128)} %get-tuple-element.255), channel_id=1, source_target_pairs={{0,4},{4,8},{8,12},{12,0},{1,5},{5,9},{9,13},{13,1},{2,6},{6,10},{... | collective-permute-start | bytes 6291464 | tf_op jit(solution)/shard_map/while/body/eval_jaxpr/ppermute | solution.py:14
  267.5 73.0 %reduce-scatter.2.cloned.1.call-start = ((), (), s32[]{:S(2)}) async-start(), calls=%async_computation.3 | async-start | bytes 3145728 | tf_op jit(solution)/shard_map/reduce_scatter | solution.py:133
Sparse Core Ops, SparseCore 0:
  9.6 11.7 all-gather.4
  23.5 81.9 all-gather.2
  267.6 60.9 all-reduce.1
  330.8 9.5 reduce-scatter.1
where the time goes:
time: 349 us
  waiting for transfers between devices  300 us (86%)
  matrix products  23.6 us (7%)
  between operations  14.7 us (4%)
  other arithmetic  6.8 us (2%)
    ppermute x3, waiting for transfers between devices, from_behind(): return lax.ppermute(x, axis, [(i, (i + by) % peers) for i in range(peers)])  145 us
    all_gather x1, waiting for transfers between devices, shards(): lax.all_gather(joined, 'section', axis=0, tiled=True)  84.1 us
    psum x1, waiting for transfers between devices, shards(): totals = lax.psum(summed, 'dp') * scale_down  52.1 us
    all_gather x1, waiting for transfers between devices, shards(): gathered = lax.all_gather(inputs, 'sub', axis=2, tiled=True)  9.36 us
    reduce_scatter x1, waiting for transfers between devices, shards(): lax.psum_scatter(partial_grad[None], 'sub', scatter_dimension=2, tiled=True)  8.55 us
    dot_general x4, matrix products, full_term(): lax.dot_general(columns, proj_grads, (((0,), (0,)), ((), ())), preferred_...  7.25 us
  transfers between devices with their start and end apart: 7, of which 7 were waited for; matrix products, arithmetic and copies ran while one was open for 4% of the time, Pallas kernels for 0%

commit v1 on v0

v1 whole, which is shorter than its diff:
```python
import functools
import math

import jax
import jax.numpy as jnp
import numpy as np
from jax import lax
from jax.experimental import pallas as pl
from jax.experimental.pallas import tpu as pltpu
from jax.sharding import PartitionSpec as P

HEAD_SIZE = 128
QUERY_GROUP = 8
BF16 = jnp.bfloat16
F32 = jnp.float32


def rotary_tables(positions_total):
    half = HEAD_SIZE // 2
    frequency = np.exp(np.arange(half) * (-2.0 * math.log(10000.0) / HEAD_SIZE))
    angles = np.arange(positions_total)[:, None] * frequency[None, :]
    cos, sin = np.cos(angles), np.sin(angles)
    return (
        np.concatenate([cos, cos], axis=1).astype(np.float32),
        np.concatenate([-sin, sin], axis=1).astype(np.float32),
    )


def repeat(start, stop, body):
    if stop - start <= 4:
        for i in range(start, stop):
            body(i)
    else:

        def step(i, carry):
            body(i)
            return carry

        lax.fori_loop(start, stop, step, 0)


def dot_nt(a, b):
    return lax.dot_general(a, b, (((1,), (1,)), ((), ())), preferred_element_type=F32)


def dot_tn(a, b):
    return lax.dot_general(a, b, (((0,), (0,)), ((), ())), preferred_element_type=F32)


def dot_nn(a, b):
    return jnp.dot(a, b, preferred_element_type=F32)


def swap_halves(a):
    half = HEAD_SIZE // 2
    return jnp.concatenate([a[:, half:], a[:, :half]], axis=1)


def kernel(
    G, S, D,
    len_ref, x_ref, q_ref, og_ref, k_ref, v_ref, cos_ref, sin_ref,
    qg_ref, ig_ref, kw_ref, vw_ref,
    wbuf, xbuf, xg, pgg, igs, igr,
    zw_s, zw_r, xw_s, xw_r, yw_s, yw_r, ax_s, ax_r, by_s, by_r,
    xs_s, xs_r, zx_s, zx_r, xx_s, xx_r, cx_s, cx_r,
    zp_s, zp_r, xp_s, xp_r, ig_s, ig_r,
):
    g, s, d, c = (lax.axis_index(a) for a in ("groups", "section", "dp", "sub"))
    T = x_ref.shape[1]
    C = k_ref.shape[1]
    R = k_ref.shape[0]
    H = S // 2
    rq = R // (G * D)
    th = T // 2
    kv = C // HEAD_SIZE
    score_scale = HEAD_SIZE ** (-0.5)

    def other_s(k):
        return lax.rem(s + k, S)

    def other_d(k):
        return lax.rem(d + k, D)

    def other_g(k):
        return lax.rem(g + k, G)

    sibling = {"sub": 1 - c}

    def rows_of(gg, dd):
        return pl.ds(pl.multiple_of((gg * D + dd) * rq, rq), rq)

    my_tokens = pl.ds(pl.multiple_of(c * th, th), th)

    def remote(src, dst, send, recv, device):
        return pltpu.make_async_remote_copy(
            src_ref=src, dst_ref=dst, send_sem=send, recv_sem=recv,
            device_id=device, device_id_type=pl.DeviceIdType.MESH,
        )

    def w_z(to, block):
        part = wbuf.at[block, rows_of(g, d)]
        return remote(part, part, zw_s.at[to], zw_r.at[block], {"section": to})

    def w_x(to, block, dd):
        part = wbuf.at[block, rows_of(g, dd)]
        return remote(part, part, xw_s.at[block, to], xw_r.at[block, dd], {"dp": to})

    def w_y(to, block, gg):
        part = wbuf.at[block, rows_of(gg, d)]
        return remote(part, part, yw_s.at[block, to], yw_r.at[block, gg], {"groups": to})

    def w_ax(to, block, gg, dd):
        part = wbuf.at[block, rows_of(gg, dd), pl.ds(0, C)]
        return remote(part, part, ax_s.at[block, gg, to], ax_r.at[block, gg, dd], {"dp": to})

    def w_by(to, block, gg, dd):
        part = wbuf.at[block, rows_of(gg, dd), pl.ds(C, C)]
        return remote(part, part, by_s.at[block, to, dd], by_r.at[block, gg, dd], {"groups": to})

    def x_sub(cc):
        part = xbuf.at[pl.ds(cc * H, H)]
        return remote(part, part, xs_s.at[0], xs_r.at[0], sibling)

    def x_z(to, owner):
        src = xbuf.at[to, my_tokens]
        dst = xg.at[owner, d, my_tokens]
        return remote(src, dst, zx_s.at[to], zx_r.at[owner], {"section": to})

    def x_x(to, block, dd):
        part = xg.at[block, dd, my_tokens]
        return remote(part, part, xx_s.at[block, to], xx_r.at[block, dd], {"dp": to})

    def x_c(cc):
        part = xg.at[:, :, pl.ds(pl.multiple_of(cc * th, th), th)]
        return remote(part, part, cx_s.at[0], cx_r.at[0], sibling)

    def p_z(to, owner):
        part = pgg.at[owner, d]
        return remote(part, part, zp_s.at[to], zp_r.at[owner], {"section": to})

    def p_x(to, block, dd):
        part = pgg.at[block, dd]
        return remote(part, part, xp_s.at[block, to], xp_r.at[block, dd], {"dp": to})

    def i_c(i):
        return remote(igs.at[i], igr.at[i], ig_s.at[i], ig_r.at[i], sibling)

    barrier = pltpu.get_barrier_semaphore()

    def greet(device):
        pl.semaphore_signal(
            barrier, inc=1, device_id=device, device_id_type=pl.DeviceIdType.MESH
        )

    greet(sibling)
    repeat(1, S, lambda k: greet({"section": other_s(k)}))
    repeat(1, D, lambda k: greet({"dp": other_d(k)}))
    repeat(1, G, lambda k: greet({"groups": other_g(k)}))
    wbuf[s, :, :C] = k_ref[...]
    wbuf[s, :, C:] = v_ref[...]
    for i in range(H):
        xbuf[c * H + i] = x_ref[0, :, i * R : (i + 1) * R]
    pl.semaphore_wait(barrier, 1 + (S - 1) + (D - 1) + (G - 1))

    x_sub(c).start()
    repeat(1, S, lambda k: w_z(other_s(k), s).start())
    x_sub(1 - c).wait_recv()
    repeat(1, S, lambda k: x_z(other_s(k), s).start())
    xg[s, d, my_tokens] = xbuf[s, my_tokens]

    def first_hand(k):
        block = other_s(k)
        w_z(block, block).wait_recv()
        repeat(1, G, lambda j: w_y(other_g(j), block, g).start())
        repeat(1, D, lambda j: w_x(other_d(j), block, d).start())

    repeat(1, S, first_hand)
    projected = dot_nn(xbuf[s], wbuf[s])

    def second_hand(k):
        block = other_s(k)

        def from_y(j):
            gg = other_g(j)
            w_y(gg, block, gg).wait_recv()
            repeat(1, D, lambda i: w_ax(other_d(i), block, gg, d).start())

        def from_x(j):
            dd = other_d(j)
            w_x(dd, block, dd).wait_recv()
            repeat(1, G, lambda i: w_by(other_g(i), block, g, dd).start())

        repeat(1, G, from_y)
        repeat(1, D, from_x)

    repeat(1, S, second_hand)

    repeat(1, D, lambda j: x_x(other_d(j), s, d).start())

    def inputs_on(k):
        block = other_s(k)
        x_z(block, block).wait_recv()
        repeat(1, D, lambda j: x_x(other_d(j), block, d).start())

    repeat(1, S, inputs_on)

    def project(k, total):
        block = other_s(k)

        def diagonal(j):
            gg = other_g(j)

            def part(i):
                dd = other_d(i)
                w_ax(dd, block, gg, dd).wait_recv()
                w_by(gg, block, gg, dd).wait_recv()

            repeat(1, D, part)

        repeat(1, G, diagonal)
        return total + dot_nn(xbuf[block], wbuf[block])

    if S <= 4:
        for k in range(1, S):
            projected = project(k, projected)
    else:
        projected = lax.fori_loop(1, S, project, projected)

    cos, sin = cos_ref[...], sin_ref[...]
    length = len_ref[0]
    u_ids = lax.broadcasted_iota(jnp.int32, (T, T), 0)
    t_ids = lax.broadcasted_iota(jnp.int32, (T, T), 1)
    allowed = (u_ids <= t_ids) & (u_ids < length)
    for h in range(kv):
        linear = projected[:, h * HEAD_SIZE : (h + 1) * HEAD_SIZE]
        keys = (linear * cos + swap_halves(linear) * sin).astype(BF16)
        values = projected[:, C + h * HEAD_SIZE : C + (h + 1) * HEAD_SIZE].astype(BF16)
        key_grad = jnp.zeros((T, HEAD_SIZE), F32)
        value_grad = jnp.zeros((T, HEAD_SIZE), F32)
        for j in range(QUERY_GROUP):
            at = slice((h * QUERY_GROUP + j) * HEAD_SIZE, (h * QUERY_GROUP + j + 1) * HEAD_SIZE)
            query, grad = q_ref[0, :, at], og_ref[0, :, at]
            scores = jnp.where(allowed, dot_nt(keys, query) * score_scale, -1e30)
            exponent = jnp.exp(scores - jnp.max(scores, axis=0, keepdims=True))
            probs = exponent / jnp.sum(exponent, axis=0, keepdims=True)
            prob_grad = dot_nt(values, grad)
            centre = jnp.sum(probs * prob_grad, axis=0, keepdims=True)
            logit_grad = (probs * (prob_grad - centre) * score_scale).astype(BF16)
            qg_ref[0, :, at] = dot_tn(logit_grad, keys).astype(BF16)
            key_grad += dot_nn(logit_grad, query)
            value_grad += dot_nn(probs.astype(BF16), grad)
        key_grad = key_grad * cos - swap_halves(key_grad) * sin
        pgg[s, d, :, h * HEAD_SIZE : (h + 1) * HEAD_SIZE] = key_grad.astype(BF16)
        pgg[s, d, :, C + h * HEAD_SIZE : C + (h + 1) * HEAD_SIZE] = value_grad.astype(BF16)

    repeat(1, S, lambda k: p_z(other_s(k), s).start())
    repeat(1, D, lambda j: p_x(other_d(j), s, d).start())
    proj_grads = pgg[s, d]
    for i in range(H):
        igs[i] = dot_nt(proj_grads, wbuf[(1 - c) * H + i])
        i_c(i).start()

    def grads_on(k):
        block = other_s(k)
        p_z(block, block).wait_recv()
        repeat(1, D, lambda j: p_x(other_d(j), block, d).start())

    repeat(1, S, grads_on)

    def inputs_in(block):
        def part(j):
            dd = other_d(j)
            x_x(dd, block, dd).wait_recv()

        repeat(1, D, part)

    repeat(0, S, inputs_in)
    x_c(c).start()
    for i in range(H):
        own = dot_nt(proj_grads, wbuf[c * H + i])
        i_c(i).wait_recv()
        ig_ref[0, :, i * R : (i + 1) * R] = (own + igr[i]).astype(BF16)

    x_c(1 - c).wait_recv()

    def grads_in(block):
        def part(j):
            dd = other_d(j)
            p_x(dd, block, dd).wait_recv()

        repeat(1, D, part)

    repeat(0, S, grads_in)

    mean = 1.0 / (S * D)
    tile = min(R, 256)
    per = D if D * T <= 512 else 1

    def weight_sum(lo, hi, first):
        for r in range(0, R, tile):
            xs = xg[lo:hi, :, :, r : r + tile].reshape((hi - lo) * D * T, tile)
            ps = pgg[lo:hi].reshape((hi - lo) * D * T, 2 * C)
            part = dot_tn(xs, ps) * mean
            kw_ref[r : r + tile] = part[:, :C]
            vw_ref[r : r + tile] = part[:, C:]

    if S * D * T <= 1024:
        weight_sum(0, S, True)
    else:
        kw_ref[...] = jnp.zeros_like(kw_ref)
        vw_ref[...] = jnp.zeros_like(vw_ref)

        def add_batch(b, carry):
            part = dot_tn(xg[b // D, lax.rem(b, D)], pgg[b // D, lax.rem(b, D)]) * mean
            kw_ref[...] += part[:, :C]
            vw_ref[...] += part[:, C:]
            return carry

        lax.fori_loop(0, S * D, add_batch, 0)

    x_sub(c).wait_send()
    x_c(c).wait_send()
    for i in range(H):
        i_c(i).wait_send()
    repeat(1, D, lambda j: x_x(other_d(j), s, d).wait_send())
    repeat(1, D, lambda j: p_x(other_d(j), s, d).wait_send())

    def sent(k):
        block = other_s(k)
        w_z(block, s).wait_send()
        x_z(block, s).wait_send()
        p_z(block, s).wait_send()

        def along_y(j):
            gg = other_g(j)
            w_y(gg, block, g).wait_send()

            def both(i):
                dd = other_d(i)
                w_ax(dd, block, gg, d).wait_send()
                w_by(gg, block, g, dd).wait_send()

            repeat(1, D, both)

        def along_x(j):
            dd = other_d(j)
            w_x(dd, block, d).wait_send()
            x_x(dd, block, d).wait_send()
            p_x(dd, block, d).wait_send()

        repeat(1, G, along_y)
        repeat(1, D, along_x)

    repeat(1, S, sent)


def shards(G, S, D, inputs, queries, out_grad, lengths, key_matrix, value_matrix):
    T = inputs.shape[1]
    R, C = key_matrix.shape
    H = S // 2
    cos, sin = rotary_tables(T)
    dma = pltpu.SemaphoreType.DMA
    vmem = pl.BlockSpec(memory_space=pltpu.VMEM)
    pairs = lambda *shape: [dma(shape), dma(shape)]
    return pl.pallas_call(
        functools.partial(kernel, G, S, D),
        out_shape=(
            jax.ShapeDtypeStruct(queries.shape, BF16),
            jax.ShapeDtypeStruct(inputs.shape, BF16),
            jax.ShapeDtypeStruct((R, C), F32),
            jax.ShapeDtypeStruct((R, C), F32),
        ),
        in_specs=[pl.BlockSpec(memory_space=pltpu.SMEM)] + [vmem] * 7,
        out_specs=(vmem,) * 4,
        scratch_shapes=[
            pltpu.VMEM((S, R, 2 * C), BF16),
            pltpu.VMEM((S, T, R), BF16),
            pltpu.VMEM((S, D, T, R), BF16),
            pltpu.VMEM((S, D, T, 2 * C), BF16),
            pltpu.VMEM((H, T, R), F32),
            pltpu.VMEM((H, T, R), F32),
            *pairs(S), *pairs(S, D), *pairs(S, G), *pairs(S, G, D), *pairs(S, G, D),
            *pairs(1), *pairs(S), *pairs(S, D), *pairs(1),
            *pairs(S), *pairs(S, D), *pairs(H),
        ],
        compiler_params=pltpu.CompilerParams(
            collective_id=0, has_side_effects=True, vmem_limit_bytes=56 * 2**20
        ),
    )(lengths, inputs, queries, out_grad, key_matrix, value_matrix, jnp.asarray(cos), jnp.asarray(sin))


def solution(mesh):
    sizes = (mesh.shape["groups"], mesh.shape["section"], mesh.shape["dp"])
    batch = P(("groups", "section", "dp"), None, "sub")
    weights = P("section", "sub")
    rows = P(("groups", "section"), "sub")
    return jax.shard_map(
        functools.partial(shards, *sizes),
        mesh=mesh,
        in_specs=(batch, batch, batch, P(("groups", "section", "dp")), weights, weights),
        out_specs=(batch, batch, rows, rows),
        check_vma=False,
    )
```

time: 349 us -> 95.6 us (0.27)
  the two profiles are of different devices: /device:TPU:0 before, /device:TPU:12 now
where the time goes in v1:
time: 95.6 us; the launch traced here: 95.3 us
  Pallas kernels  87.6 us (92%)
  local copies, waits for them, and re-layouts  6.43 us (7%)
  between operations  1.3 us (1%)
    pallas_call x1, Pallas kernels, shards(): pl.pallas_call(functools.partial(kernel, G, S, D), out_shape=(jax.ShapeDt...  87.6 us
    unnamed x8, local copies, waits for them, and re-layouts  6.43 us

profile of v1, /device:TPU:12, one launch (start us, length us, event | category | flops | bytes accessed | tf_op | source)
XLA Modules:
  0.0 95.3 jit_solution(15150758408207012922)
XLA Ops:
  1.3 87.6 %shard_map.111 = (bf16[1,128,2048]{2,1,0:T(8,128)(2,1)}, bf16[1,128,2048]{2,1,0:T(8,128)(2,1)}, f32[1024,256]{1,0:T(8,128)}, f32[1024,256]{1,0:T(8,128)}) custom-call(s32[1]{0:T(128)S(6)} %copy.16.len_ref, bf16[1,128,2048]{2,1,0:T(8,128)(2,1)} %x_ref.1, bf16[1,128,2048]{2,1,0:T(8,128)(2,1)} %q_ref.1, bf16[1,128,2048]{2,1,0:T(8,128)(2,1)} %og_ref.1, ...), custom_call_target="tpu_custom_call" | custom-call | tf_op jit(solution)/shard_map/pallas_call | solution.py:365
  88.9 0.0 copy-start.1
  88.9 2.0 %copy.17 = bf16[1,128,2048]{2,1,0:T(8,128)(2,1)} copy(bf16[1,128,2048]{2,1,0:T(8,128)(2,1)} %get-tuple-element.8) | data formatting | bytes 1048576
  90.8 1.9 %copy.18 = bf16[1,128,2048]{2,1,0:T(8,128)(2,1)} copy(bf16[1,128,2048]{2,1,0:T(8,128)(2,1)} %get-tuple-element.9) | data formatting | bytes 1048576
  92.7 0.0 copy-done.1
  92.7 0.0 copy-start
  92.7 1.0 %copy.19 = f32[1024,256]{1,0:T(8,128)} copy(f32[1024,256]{1,0:T(8,128)S(1)} %copy-done.1) | data formatting | bytes 2097152
  93.7 0.6 copy-done
  94.3 1.0 %copy.20 = f32[1024,256]{1,0:T(8,128)} copy(f32[1024,256]{1,0:T(8,128)S(1)} %copy-done) | data formatting | bytes 2097152
Async XLA Ops:
  88.9 3.9 %copy-start.1 = (f32[1024,256]{1,0:T(8,128)S(1)}, f32[1024,256]{1,0:T(8,128)}, u32[]{:S(2)}) copy-start(f32[1024,256]{1,0:T(8,128)} %get-tuple-element.10) | copy-start | bytes 3145732
  92.7 1.6 %copy-start = (f32[1024,256]{1,0:T(8,128)S(1)}, f32[1024,256]{1,0:T(8,128)}, u32[]{:S(2)}) copy-start(f32[1024,256]{1,0:T(8,128)} %get-tuple-element.11) | copy-start | bytes 3145732

commit v2 on v1

--- a/solution.py
+++ b/solution.py
@@ -60,7 +60,7 @@
     G, S, D,
     len_ref, x_ref, q_ref, og_ref, k_ref, v_ref, cos_ref, sin_ref,
     qg_ref, ig_ref, kw_ref, vw_ref,
-    wbuf, xbuf, xg, pgg, igs, igr,
+    wbuf, xbuf, xg, pgg, igs, igr, projected,
     zw_s, zw_r, xw_s, xw_r, yw_s, yw_r, ax_s, ax_r, by_s, by_r,
     xs_s, xs_r, zx_s, zx_r, xx_s, xx_r, cx_s, cx_r,
     zp_s, zp_r, xp_s, xp_r, ig_s, ig_r,
@@ -97,24 +97,27 @@
             device_id=device, device_id_type=pl.DeviceIdType.MESH,
         )
 
-    def w_z(to, block):
-        part = wbuf.at[block, rows_of(g, d)]
-        return remote(part, part, zw_s.at[to], zw_r.at[block], {"section": to})
-
-    def w_x(to, block, dd):
-        part = wbuf.at[block, rows_of(g, dd)]
-        return remote(part, part, xw_s.at[block, to], xw_r.at[block, dd], {"dp": to})
-
-    def w_y(to, block, gg):
-        part = wbuf.at[block, rows_of(gg, d)]
-        return remote(part, part, yw_s.at[block, to], yw_r.at[block, gg], {"groups": to})
+    def half_of(half):
+        return pl.ds(half * C, C)
+
+    def w_z(to, way, block, half):
+        part = wbuf.at[block, rows_of(g, d), half_of(half)]
+        return remote(part, part, zw_s.at[way, block, half], zw_r.at[block, half], {"section": to})
+
+    def w_x(to, block, dd, half):
+        part = wbuf.at[block, rows_of(g, dd), half_of(half)]
+        return remote(part, part, xw_s.at[block, to, half], xw_r.at[block, dd, half], {"dp": to})
+
+    def w_y(to, block, gg, half):
+        part = wbuf.at[block, rows_of(gg, d), half_of(half)]
+        return remote(part, part, yw_s.at[block, to, half], yw_r.at[block, gg, half], {"groups": to})
 
     def w_ax(to, block, gg, dd):
-        part = wbuf.at[block, rows_of(gg, dd), pl.ds(0, C)]
+        part = wbuf.at[block, rows_of(gg, dd), half_of(0)]
         return remote(part, part, ax_s.at[block, gg, to], ax_r.at[block, gg, dd], {"dp": to})
 
     def w_by(to, block, gg, dd):
-        part = wbuf.at[block, rows_of(gg, dd), pl.ds(C, C)]
+        part = wbuf.at[block, rows_of(gg, dd), half_of(1)]
         return remote(part, part, by_s.at[block, to, dd], by_r.at[block, gg, dd], {"groups": to})
 
     def x_sub(cc):
@@ -134,9 +137,9 @@
         part = xg.at[:, :, pl.ds(pl.multiple_of(cc * th, th), th)]
         return remote(part, part, cx_s.at[0], cx_r.at[0], sibling)
 
-    def p_z(to, owner):
+    def p_z(to, way, owner):
         part = pgg.at[owner, d]
-        return remote(part, part, zp_s.at[to], zp_r.at[owner], {"section": to})
+        return remote(part, part, zp_s.at[way, owner], zp_r.at[owner], {"section": to})
 
     def p_x(to, block, dd):
         part = pgg.at[block, dd]
@@ -162,40 +165,85 @@
         xbuf[c * H + i] = x_ref[0, :, i * R : (i + 1) * R]
     pl.semaphore_wait(barrier, 1 + (S - 1) + (D - 1) + (G - 1))
 
+    def along_line(k, body):
+        @pl.when(s >= k)
+        def _():
+            body(s - k, 0, s < S - 1, s + 1)
+
+        @pl.when(s + k < S)
+        def _():
+            body(s + k, 1, s > 0, s - 1)
+
+    def both_ways(body):
+        @pl.when(s < S - 1)
+        def _():
+            body(s + 1, 0)
+
+        @pl.when(s > 0)
+        def _():
+            body(s - 1, 1)
+
     x_sub(c).start()
-    repeat(1, S, lambda k: w_z(other_s(k), s).start())
+    for half in range(2):
+        both_ways(lambda to, way: w_z(to, way, s, half).start())
     x_sub(1 - c).wait_recv()
+    xg[s, d, my_tokens] = xbuf[s, my_tokens]
+    projected[...] = dot_nn(xbuf[s], wbuf[s])
+
+    def first_hand(block, way, more, to):
+        for half in range(2):
+            w_z(s, way, block, half).wait_recv()
+
+            @pl.when(more)
+            def _():
+                w_z(to, way, block, half).start()
+
+            repeat(1, G, lambda j: w_y(other_g(j), block, g, half).start())
+            repeat(1, D, lambda j: w_x(other_d(j), block, d, half).start())
+
+    def second_hand(block, way, more, to):
+        for half in range(2):
+
+            def from_y(j):
+                gg = other_g(j)
+                w_y(gg, block, gg, half).wait_recv()
+                if half == 0:
+                    repeat(1, D, lambda i: w_ax(other_d(i), block, gg, d).start())
+
+            def from_x(j):
+                dd = other_d(j)
+                w_x(dd, block, dd, half).wait_recv()
+                if half == 1:
+                    repeat(1, G, lambda i: w_by(other_g(i), block, g, dd).start())
+
+            repeat(1, G, from_y)
+            repeat(1, D, from_x)
+
+    def project(block, way, more, to):
+        def diagonal(j):
+            gg = other_g(j)
+
+            def part(i):
+                dd = other_d(i)
+                w_ax(dd, block, gg, dd).wait_recv()
+                w_by(gg, block, gg, dd).wait_recv()
+
+            repeat(1, D, part)
+
+        repeat(1, G, diagonal)
+        projected[...] += dot_nn(xbuf[block], wbuf[block])
+
+    along_line(1, first_hand)
+
+    def hop(k):
+        along_line(k, first_hand)
+        along_line(k - 1, second_hand)
+
+    repeat(2, S, hop)
     repeat(1, S, lambda k: x_z(other_s(k), s).start())
-    xg[s, d, my_tokens] = xbuf[s, my_tokens]
-
-    def first_hand(k):
-        block = other_s(k)
-        w_z(block, block).wait_recv()
-        repeat(1, G, lambda j: w_y(other_g(j), block, g).start())
-        repeat(1, D, lambda j: w_x(other_d(j), block, d).start())
-
-    repeat(1, S, first_hand)
-    projected = dot_nn(xbuf[s], wbuf[s])
-
-    def second_hand(k):
-        block = other_s(k)
-
-        def from_y(j):
-            gg = other_g(j)
-            w_y(gg, block, gg).wait_recv()
-            repeat(1, D, lambda i: w_ax(other_d(i), block, gg, d).start())
-
-        def from_x(j):
-            dd = other_d(j)
-            w_x(dd, block, dd).wait_recv()
-            repeat(1, G, lambda i: w_by(other_g(i), block, g, dd).start())
-
-        repeat(1, G, from_y)
-        repeat(1, D, from_x)
-
-    repeat(1, S, second_hand)
-
+    along_line(S - 1, second_hand)
     repeat(1, D, lambda j: x_x(other_d(j), s, d).start())
+    repeat(1, S, lambda k: along_line(k, project))
 
     def inputs_on(k):
         block = other_s(k)
@@ -203,28 +251,6 @@
         repeat(1, D, lambda j: x_x(other_d(j), block, d).start())
 
     repeat(1, S, inputs_on)
-
-    def project(k, total):
-        block = other_s(k)
-
-        def diagonal(j):
-            gg = other_g(j)
-
-            def part(i):
-                dd = other_d(i)
-                w_ax(dd, block, gg, dd).wait_recv()
-                w_by(gg, block, gg, dd).wait_recv()
-
-            repeat(1, D, part)
-
-        repeat(1, G, diagonal)
-        return total + dot_nn(xbuf[block], wbuf[block])
-
-    if S <= 4:
-        for k in range(1, S):
-            projected = project(k, projected)
-    else:
-        projected = lax.fori_loop(1, S, project, projected)
 
     cos, sin = cos_ref[...], sin_ref[...]
     length = len_ref[0]
@@ -253,19 +279,23 @@
         pgg[s, d, :, h * HEAD_SIZE : (h + 1) * HEAD_SIZE] = key_grad.astype(BF16)
         pgg[s, d, :, C + h * HEAD_SIZE : C + (h + 1) * HEAD_SIZE] = value_grad.astype(BF16)
 
-    repeat(1, S, lambda k: p_z(other_s(k), s).start())
+    both_ways(lambda to, way: p_z(to, way, s).start())
     repeat(1, D, lambda j: p_x(other_d(j), s, d).start())
     proj_grads = pgg[s, d]
     for i in range(H):
         igs[i] = dot_nt(proj_grads, wbuf[(1 - c) * H + i])
         i_c(i).start()
 
-    def grads_on(k):
-        block = other_s(k)
-        p_z(block, block).wait_recv()
+    def grads_on(block, way, more, to):
+        p_z(s, way, block).wait_recv()
+
+        @pl.when(more)
+        def _():
+            p_z(to, way, block).start()
+
         repeat(1, D, lambda j: p_x(other_d(j), block, d).start())
 
-    repeat(1, S, grads_on)
+    repeat(1, S, lambda k: along_line(k, grads_on))
 
     def inputs_in(block):
         def part(j):
@@ -325,15 +355,24 @@
     repeat(1, D, lambda j: x_x(other_d(j), s, d).wait_send())
     repeat(1, D, lambda j: p_x(other_d(j), s, d).wait_send())
 
-    def sent(k):
-        block = other_s(k)
-        w_z(block, s).wait_send()
+    def line_sent(to, way, block):
+        for half in range(2):
+            w_z(to, way, block, half).wait_send()
+        p_z(to, way, block).wait_send()
+
+    both_ways(lambda to, way: line_sent(to, way, s))
+
+    def sent(block, way, more, to):
+        @pl.when(more)
+        def _():
+            line_sent(to, way, block)
+
         x_z(block, s).wait_send()
-        p_z(block, s).wait_send()
 
         def along_y(j):
             gg = other_g(j)
-            w_y(gg, block, g).wait_send()
+            for half in range(2):
+                w_y(gg, block, g, half).wait_send()
 
             def both(i):
                 dd = other_d(i)
@@ -344,14 +383,15 @@
 
         def along_x(j):
             dd = other_d(j)
-            w_x(dd, block, d).wait_send()
+            for half in range(2):
+                w_x(dd, block, d, half).wait_send()
             x_x(dd, block, d).wait_send()
             p_x(dd, block, d).wait_send()
 
         repeat(1, G, along_y)
         repeat(1, D, along_x)
 
-    repeat(1, S, sent)
+    repeat(1, S, lambda k: along_line(k, sent))
 
 
 def shards(G, S, D, inputs, queries, out_grad, lengths, key_matrix, value_matrix):
@@ -379,9 +419,10 @@
             pltpu.VMEM((S, D, T, 2 * C), BF16),
             pltpu.VMEM((H, T, R), F32),
             pltpu.VMEM((H, T, R), F32),
-            *pairs(S), *pairs(S, D), *pairs(S, G), *pairs(S, G, D), *pairs(S, G, D),
+            pltpu.VMEM((T, 2 * C), F32),
+            dma((2, S, 2)), dma((S, 2)), *pairs(S, D, 2), *pairs(S, G, 2), *pairs(S, G, D), *pairs(S, G, D),
             *pairs(1), *pairs(S), *pairs(S, D), *pairs(1),
-            *pairs(S), *pairs(S, D), *pairs(H),
+            dma((2, S)), dma((S,)), *pairs(S, D), *pairs(H),
         ],
         compiler_params=pltpu.CompilerParams(
             collective_id=0, has_side_effects=True, vmem_limit_bytes=56 * 2**20

time: 95.6 us -> 74.6 us (0.78)
  the two profiles are of different devices: /device:TPU:12 before, /device:TPU:0 now
where the time goes in v2:
time: 74.6 us; the launch traced here: 74.4 us
  Pallas kernels  66.6 us (89%)
  local copies, waits for them, and re-layouts  6.43 us (9%)
  between operations  1.3 us (2%)
    pallas_call x1, Pallas kernels, shards(): pl.pallas_call(functools.partial(kernel, G, S, D), out_shape=(jax.ShapeDt...  66.6 us
    unnamed x8, local copies, waits for them, and re-layouts  6.43 us

profile of v2, /device:TPU:0, one launch (start us, length us, event | category | flops | bytes accessed | tf_op | source)
XLA Modules:
  0.0 74.4 jit_solution(3753187232378018609)
XLA Ops:
  1.3 66.6 %shard_map.111 = (bf16[1,128,2048]{2,1,0:T(8,128)(2,1)}, bf16[1,128,2048]{2,1,0:T(8,128)(2,1)}, f32[1024,256]{1,0:T(8,128)}, f32[1024,256]{1,0:T(8,128)}) custom-call(s32[1]{0:T(128)S(6)} %copy.16.len_ref, bf16[1,128,2048]{2,1,0:T(8,128)(2,1)} %x_ref.1, bf16[1,128,2048]{2,1,0:T(8,128)(2,1)} %q_ref.1, bf16[1,128,2048]{2,1,0:T(8,128)(2,1)} %og_ref.1, ...), custom_call_target="tpu_custom_call" | custom-call | tf_op jit(solution)/shard_map/pallas_call | solution.py:405
  67.9 0.0 copy-start.1
  67.9 2.0 %copy.17 = bf16[1,128,2048]{2,1,0:T(8,128)(2,1)} copy(bf16[1,128,2048]{2,1,0:T(8,128)(2,1)} %get-tuple-element.8) | data formatting | bytes 1048576
  69.9 1.9 %copy.18 = bf16[1,128,2048]{2,1,0:T(8,128)(2,1)} copy(bf16[1,128,2048]{2,1,0:T(8,128)(2,1)} %get-tuple-element.9) | data formatting | bytes 1048576
  71.8 0.0 copy-done.1
  71.8 0.0 copy-start
  71.8 1.0 %copy.19 = f32[1024,256]{1,0:T(8,128)} copy(f32[1024,256]{1,0:T(8,128)S(1)} %copy-done.1) | data formatting | bytes 2097152
  72.8 0.6 copy-done
  73.4 1.0 %copy.20 = f32[1024,256]{1,0:T(8,128)} copy(f32[1024,256]{1,0:T(8,128)S(1)} %copy-done) | data formatting | bytes 2097152
Async XLA Ops:
  67.9 3.9 %copy-start.1 = (f32[1024,256]{1,0:T(8,128)S(1)}, f32[1024,256]{1,0:T(8,128)}, u32[]{:S(2)}) copy-start(f32[1024,256]{1,0:T(8,128)} %get-tuple-element.10) | copy-start | bytes 3145732
  71.8 1.6 %copy-start = (f32[1024,256]{1,0:T(8,128)S(1)}, f32[1024,256]{1,0:T(8,128)}, u32[]{:S(2)}) copy-start(f32[1024,256]{1,0:T(8,128)} %get-tuple-element.11) | copy-start | bytes 3145732

commit v3 on v2

--- a/solution.py
+++ b/solution.py
@@ -11,6 +11,7 @@
 
 HEAD_SIZE = 128
 QUERY_GROUP = 8
+CHUNKS = 2
 BF16 = jnp.bfloat16
 F32 = jnp.float32
 
@@ -97,28 +98,25 @@
             device_id=device, device_id_type=pl.DeviceIdType.MESH,
         )
 
-    def half_of(half):
-        return pl.ds(half * C, C)
-
     def w_z(to, way, block, half):
-        part = wbuf.at[block, rows_of(g, d), half_of(half)]
+        part = wbuf.at[block, half, rows_of(g, d)]
         return remote(part, part, zw_s.at[way, block, half], zw_r.at[block, half], {"section": to})
 
     def w_x(to, block, dd, half):
-        part = wbuf.at[block, rows_of(g, dd), half_of(half)]
+        part = wbuf.at[block, half, rows_of(g, dd)]
         return remote(part, part, xw_s.at[block, to, half], xw_r.at[block, dd, half], {"dp": to})
 
     def w_y(to, block, gg, half):
-        part = wbuf.at[block, rows_of(gg, d), half_of(half)]
+        part = wbuf.at[block, half, rows_of(gg, d)]
         return remote(part, part, yw_s.at[block, to, half], yw_r.at[block, gg, half], {"groups": to})
 
-    def w_ax(to, block, gg, dd):
-        part = wbuf.at[block, rows_of(gg, dd), half_of(0)]
-        return remote(part, part, ax_s.at[block, gg, to], ax_r.at[block, gg, dd], {"dp": to})
-
-    def w_by(to, block, gg, dd):
-        part = wbuf.at[block, rows_of(gg, dd), half_of(1)]
-        return remote(part, part, by_s.at[block, to, dd], by_r.at[block, gg, dd], {"groups": to})
+    def w_ax(to, block, gg, dd, half):
+        part = wbuf.at[block, half, rows_of(gg, dd)]
+        return remote(part, part, ax_s.at[block, gg, to, half], ax_r.at[block, gg, dd, half], {"dp": to})
+
+    def w_by(to, block, gg, dd, half):
+        part = wbuf.at[block, half, rows_of(gg, dd)]
+        return remote(part, part, by_s.at[block, to, dd, half], by_r.at[block, gg, dd, half], {"groups": to})
 
     def x_sub(cc):
         part = xbuf.at[pl.ds(cc * H, H)]
@@ -137,13 +135,13 @@
         part = xg.at[:, :, pl.ds(pl.multiple_of(cc * th, th), th)]
         return remote(part, part, cx_s.at[0], cx_r.at[0], sibling)
 
-    def p_z(to, way, owner):
-        part = pgg.at[owner, d]
-        return remote(part, part, zp_s.at[way, owner], zp_r.at[owner], {"section": to})
-
-    def p_x(to, block, dd):
-        part = pgg.at[block, dd]
-        return remote(part, part, xp_s.at[block, to], xp_r.at[block, dd], {"dp": to})
+    def p_z(to, way, owner, h):
+        part = pgg.at[owner, d, h]
+        return remote(part, part, zp_s.at[way, owner, h], zp_r.at[owner, h], {"section": to})
+
+    def p_x(to, block, dd, h):
+        part = pgg.at[block, dd, h]
+        return remote(part, part, xp_s.at[block, to, h], xp_r.at[block, dd, h], {"dp": to})
 
     def i_c(i):
         return remote(igs.at[i], igr.at[i], ig_s.at[i], ig_r.at[i], sibling)
@@ -159,8 +157,8 @@
     repeat(1, S, lambda k: greet({"section": other_s(k)}))
     repeat(1, D, lambda k: greet({"dp": other_d(k)}))
     repeat(1, G, lambda k: greet({"groups": other_g(k)}))
-    wbuf[s, :, :C] = k_ref[...]
-    wbuf[s, :, C:] = v_ref[...]
+    wbuf[s, 0] = k_ref[...]
+    wbuf[s, 1] = v_ref[...]
     for i in range(H):
         xbuf[c * H + i] = x_ref[0, :, i * R : (i + 1) * R]
     pl.semaphore_wait(barrier, 1 + (S - 1) + (D - 1) + (G - 1))
@@ -184,14 +182,16 @@
             body(s - 1, 1)
 
     x_sub(c).start()
-    for half in range(2):
+    for half in range(CHUNKS):
         both_ways(lambda to, way: w_z(to, way, s, half).start())
     x_sub(1 - c).wait_recv()
     xg[s, d, my_tokens] = xbuf[s, my_tokens]
-    projected[...] = dot_nn(xbuf[s], wbuf[s])
+    repeat(1, D, lambda j: x_x(other_d(j), s, d).start())
+    projected[:, :C] = dot_nn(xbuf[s], wbuf[s, 0])
+    projected[:, C:] = dot_nn(xbuf[s], wbuf[s, 1])
 
     def first_hand(block, way, more, to):
-        for half in range(2):
+        for half in range(CHUNKS):
             w_z(s, way, block, half).wait_recv()
 
             @pl.when(more)
@@ -202,19 +202,19 @@
             repeat(1, D, lambda j: w_x(other_d(j), block, d, half).start())
 
     def second_hand(block, way, more, to):
-        for half in range(2):
+        for half in range(CHUNKS):
 
             def from_y(j):
                 gg = other_g(j)
                 w_y(gg, block, gg, half).wait_recv()
-                if half == 0:
-                    repeat(1, D, lambda i: w_ax(other_d(i), block, gg, d).start())
+                if half < CHUNKS // 2:
+                    repeat(1, D, lambda i: w_ax(other_d(i), block, gg, d, half).start())
 
             def from_x(j):
                 dd = other_d(j)
                 w_x(dd, block, dd, half).wait_recv()
-                if half == 1:
-                    repeat(1, G, lambda i: w_by(other_g(i), block, g, dd).start())
+                if half >= CHUNKS // 2:
+                    repeat(1, G, lambda i: w_by(other_g(i), block, g, dd, half).start())
 
             repeat(1, G, from_y)
             repeat(1, D, from_x)
@@ -225,13 +225,16 @@
 
             def part(i):
                 dd = other_d(i)
-                w_ax(dd, block, gg, dd).wait_recv()
-                w_by(gg, block, gg, dd).wait_recv()
+                for half in range(CHUNKS // 2):
+                    w_ax(dd, block, gg, dd, half).wait_recv()
+                for half in range(CHUNKS // 2, CHUNKS):
+                    w_by(gg, block, gg, dd, half).wait_recv()
 
             repeat(1, D, part)
 
         repeat(1, G, diagonal)
-        projected[...] += dot_nn(xbuf[block], wbuf[block])
+        projected[:, :C] += dot_nn(xbuf[block], wbuf[block, 0])
+        projected[:, C:] += dot_nn(xbuf[block], wbuf[block, 1])
 
     along_line(1, first_hand)
 
@@ -242,14 +245,13 @@
     repeat(2, S, hop)
     repeat(1, S, lambda k: x_z(other_s(k), s).start())
     along_line(S - 1, second_hand)
-    repeat(1, D, lambda j: x_x(other_d(j), s, d).start())
-    repeat(1, S, lambda k: along_line(k, project))
 
     def inputs_on(k):
         block = other_s(k)
         x_z(block, block).wait_recv()
         repeat(1, D, lambda j: x_x(other_d(j), block, d).start())
 
+    repeat(1, S, lambda k: along_line(k, project))
     repeat(1, S, inputs_on)
 
     cos, sin = cos_ref[...], sin_ref[...]
@@ -276,24 +278,34 @@
             key_grad += dot_nn(logit_grad, query)
             value_grad += dot_nn(probs.astype(BF16), grad)
         key_grad = key_grad * cos - swap_halves(key_grad) * sin
-        pgg[s, d, :, h * HEAD_SIZE : (h + 1) * HEAD_SIZE] = key_grad.astype(BF16)
-        pgg[s, d, :, C + h * HEAD_SIZE : C + (h + 1) * HEAD_SIZE] = value_grad.astype(BF16)
-
-    both_ways(lambda to, way: p_z(to, way, s).start())
-    repeat(1, D, lambda j: p_x(other_d(j), s, d).start())
-    proj_grads = pgg[s, d]
+        pgg[s, d, h, :, :HEAD_SIZE] = key_grad.astype(BF16)
+        pgg[s, d, h, :, HEAD_SIZE:] = value_grad.astype(BF16)
+        both_ways(lambda to, way: p_z(to, way, s, h).start())
+        repeat(1, D, lambda j: p_x(other_d(j), s, d, h).start())
+
+    def by_matrix(parts):
+        return jnp.concatenate(
+            [p[:, :HEAD_SIZE] for p in parts] + [p[:, HEAD_SIZE:] for p in parts], axis=1
+        )
+
+    proj_grads = by_matrix([pgg[s, d, h] for h in range(kv)])
+
+    def input_part(block):
+        return dot_nt(proj_grads[:, :C], wbuf[block, 0]) + dot_nt(proj_grads[:, C:], wbuf[block, 1])
+
     for i in range(H):
-        igs[i] = dot_nt(proj_grads, wbuf[(1 - c) * H + i])
+        igs[i] = input_part((1 - c) * H + i)
         i_c(i).start()
 
     def grads_on(block, way, more, to):
-        p_z(s, way, block).wait_recv()
-
-        @pl.when(more)
-        def _():
-            p_z(to, way, block).start()
-
-        repeat(1, D, lambda j: p_x(other_d(j), block, d).start())
+        for h in range(kv):
+            p_z(s, way, block, h).wait_recv()
+
+            @pl.when(more)
+            def _():
+                p_z(to, way, block, h).start()
+
+            repeat(1, D, lambda j: p_x(other_d(j), block, d, h).start())
 
     repeat(1, S, lambda k: along_line(k, grads_on))
 
@@ -307,7 +319,7 @@
     repeat(0, S, inputs_in)
     x_c(c).start()
     for i in range(H):
-        own = dot_nt(proj_grads, wbuf[c * H + i])
+        own = input_part(c * H + i)
         i_c(i).wait_recv()
         ig_ref[0, :, i * R : (i + 1) * R] = (own + igr[i]).astype(BF16)
 
@@ -316,7 +328,8 @@
     def grads_in(block):
         def part(j):
             dd = other_d(j)
-            p_x(dd, block, dd).wait_recv()
+            for h in range(kv):
+                p_x(dd, block, dd, h).wait_recv()
 
         repeat(1, D, part)
 
@@ -324,26 +337,25 @@
 
     mean = 1.0 / (S * D)
     tile = min(R, 256)
-    per = D if D * T <= 512 else 1
-
-    def weight_sum(lo, hi, first):
-        for r in range(0, R, tile):
-            xs = xg[lo:hi, :, :, r : r + tile].reshape((hi - lo) * D * T, tile)
-            ps = pgg[lo:hi].reshape((hi - lo) * D * T, 2 * C)
-            part = dot_tn(xs, ps) * mean
-            kw_ref[r : r + tile] = part[:, :C]
-            vw_ref[r : r + tile] = part[:, C:]
-
     if S * D * T <= 1024:
-        weight_sum(0, S, True)
+        for h in range(kv):
+            at = slice(h * HEAD_SIZE, (h + 1) * HEAD_SIZE)
+            ps = pgg[:, :, h].reshape(S * D * T, 2 * HEAD_SIZE)
+            for r in range(0, R, tile):
+                xs = xg[:, :, :, r : r + tile].reshape(S * D * T, tile)
+                part = dot_tn(xs, ps) * mean
+                kw_ref[r : r + tile, at] = part[:, :HEAD_SIZE]
+                vw_ref[r : r + tile, at] = part[:, HEAD_SIZE:]
     else:
         kw_ref[...] = jnp.zeros_like(kw_ref)
         vw_ref[...] = jnp.zeros_like(vw_ref)
 
         def add_batch(b, carry):
-            part = dot_tn(xg[b // D, lax.rem(b, D)], pgg[b // D, lax.rem(b, D)]) * mean
-            kw_ref[...] += part[:, :C]
-            vw_ref[...] += part[:, C:]
+            for h in range(kv):
+                at = slice(h * HEAD_SIZE, (h + 1) * HEAD_SIZE)
+                part = dot_tn(xg[b // D, lax.rem(b, D)], pgg[b // D, lax.rem(b, D), h]) * mean
+                kw_ref[:, at] += part[:, :HEAD_SIZE]
+                vw_ref[:, at] += part[:, HEAD_SIZE:]
             return carry
 
         lax.fori_loop(0, S * D, add_batch, 0)
@@ -353,12 +365,14 @@
     for i in range(H):
         i_c(i).wait_send()
     repeat(1, D, lambda j: x_x(other_d(j), s, d).wait_send())
-    repeat(1, D, lambda j: p_x(other_d(j), s, d).wait_send())
+    for h in range(kv):
+        repeat(1, D, lambda j: p_x(other_d(j), s, d, h).wait_send())
 
     def line_sent(to, way, block):
-        for half in range(2):
+        for half in range(CHUNKS):
             w_z(to, way, block, half).wait_send()
-        p_z(to, way, block).wait_send()
+        for h in range(kv):
+            p_z(to, way, block, h).wait_send()
 
     both_ways(lambda to, way: line_sent(to, way, s))
 
@@ -371,38 +385,55 @@
 
         def along_y(j):
             gg = other_g(j)
-            for half in range(2):
+            for half in range(CHUNKS):
                 w_y(gg, block, g, half).wait_send()
 
             def both(i):
                 dd = other_d(i)
-                w_ax(dd, block, gg, d).wait_send()
-                w_by(gg, block, g, dd).wait_send()
+                for half in range(CHUNKS // 2):
+                    w_ax(dd, block, gg, d, half).wait_send()
+                for half in range(CHUNKS // 2, CHUNKS):
+                    w_by(gg, block, g, dd, half).wait_send()
 
             repeat(1, D, both)
 
         def along_x(j):
             dd = other_d(j)
-            for half in range(2):
+            for half in range(CHUNKS):
                 w_x(dd, block, d, half).wait_send()
             x_x(dd, block, d).wait_send()
-            p_x(dd, block, d).wait_send()
+            for h in range(kv):
+                p_x(dd, block, d, h).wait_send()
 
         repeat(1, G, along_y)
         repeat(1, D, along_x)
 
     repeat(1, S, lambda k: along_line(k, sent))
+
+
+def hand_out(*refs):
+    ins, outs, held, sems = refs[:4], refs[4:8], refs[8:12], refs[12]
+    loads = [pltpu.make_async_copy(ins[i], held[i], sems.at[0, i]) for i in range(4)]
+    stores = [pltpu.make_async_copy(held[i], outs[i], sems.at[1, i]) for i in range(4)]
+    for load in loads:
+        load.start()
+    for load, store in zip(loads, stores):
+        load.wait()
+        store.start()
+    for store in stores:
+        store.wait()
 
 
 def shards(G, S, D, inputs, queries, out_grad, lengths, key_matrix, value_matrix):
     T = inputs.shape[1]
     R, C = key_matrix.shape
     H = S // 2
+    kv = C // HEAD_SIZE
     cos, sin = rotary_tables(T)
     dma = pltpu.SemaphoreType.DMA
     vmem = pl.BlockSpec(memory_space=pltpu.VMEM)
     pairs = lambda *shape: [dma(shape), dma(shape)]
-    return pl.pallas_call(
+    results = pl.pallas_call(
         functools.partial(kernel, G, S, D),
         out_shape=(
             jax.ShapeDtypeStruct(queries.shape, BF16),
@@ -413,21 +444,30 @@
         in_specs=[pl.BlockSpec(memory_space=pltpu.SMEM)] + [vmem] * 7,
         out_specs=(vmem,) * 4,
         scratch_shapes=[
-            pltpu.VMEM((S, R, 2 * C), BF16),
+            pltpu.VMEM((S, CHUNKS, R, C), BF16),
             pltpu.VMEM((S, T, R), BF16),
             pltpu.VMEM((S, D, T, R), BF16),
-            pltpu.VMEM((S, D, T, 2 * C), BF16),
+            pltpu.VMEM((S, D, kv, T, 2 * HEAD_SIZE), BF16),
             pltpu.VMEM((H, T, R), F32),
             pltpu.VMEM((H, T, R), F32),
             pltpu.VMEM((T, 2 * C), F32),
-            dma((2, S, 2)), dma((S, 2)), *pairs(S, D, 2), *pairs(S, G, 2), *pairs(S, G, D), *pairs(S, G, D),
+            dma((2, S, CHUNKS)), dma((S, CHUNKS)), *pairs(S, D, CHUNKS), *pairs(S, G, CHUNKS),
+            *pairs(S, G, D, CHUNKS), *pairs(S, G, D, CHUNKS),
             *pairs(1), *pairs(S), *pairs(S, D), *pairs(1),
-            dma((2, S)), dma((S,)), *pairs(S, D), *pairs(H),
+            dma((2, S, kv)), dma((S, kv)), *pairs(S, D, kv), *pairs(H),
         ],
         compiler_params=pltpu.CompilerParams(
             collective_id=0, has_side_effects=True, vmem_limit_bytes=56 * 2**20
         ),
     )(lengths, inputs, queries, out_grad, key_matrix, value_matrix, jnp.asarray(cos), jnp.asarray(sin))
+    anywhere = pl.BlockSpec(memory_space=pl.ANY)
+    return pl.pallas_call(
+        hand_out,
+        out_shape=tuple(jax.ShapeDtypeStruct(r.shape, r.dtype) for r in results),
+        in_specs=[anywhere] * 4,
+        out_specs=(anywhere,) * 4,
+        scratch_shapes=[*(pltpu.VMEM(r.shape, r.dtype) for r in results), dma((2, 4))],
+    )(*results)
 
 
 def solution(mesh):

time: 74.6 us -> 69.1 us (0.926)
  local copies, waits for them, and re-layouts: 6.43 us -> 0 us
  Pallas kernels: 66.6 us -> 67.6 us
    unnamed x8 -> x0, local copies, waits for them, and re-layouts: 6.43 us -> none
    pallas_call x0 -> x1, Pallas kernels: none -> 2.93 us  [shards(): pl.pallas_call(hand_out, out_shape=tuple((jax.ShapeDtypeStruct(r.shape, r...]
    pallas_call x1, Pallas kernels: 66.6 us -> 64.7 us  [shards(): pl.pallas_call(functools.partial(kernel, G, S, D), out_shape=(jax.ShapeDt...]
where the time goes in v3:
time: 69.1 us; the launch traced here: 68.9 us
  Pallas kernels  67.6 us (98%)
  between operations  1.29 us (2%)
    pallas_call x1, Pallas kernels, shards(): pl.pallas_call(functools.partial(kernel, G, S, D), out_shape=(jax.ShapeDt...  64.7 us
    pallas_call x1, Pallas kernels, shards(): pl.pallas_call(hand_out, out_shape=tuple((jax.ShapeDtypeStruct(r.shape, r...  2.93 us

profile of v3, /device:TPU:0, one launch (start us, length us, event | category | flops | bytes accessed | tf_op | source)
XLA Modules:
  0.0 68.9 jit_solution(2639786892024067767)
XLA Ops:
  1.3 64.7 %shard_map.111 = (bf16[1,128,2048]{2,1,0:T(8,128)(2,1)}, bf16[1,128,2048]{2,1,0:T(8,128)(2,1)}, f32[1024,256]{1,0:T(8,128)}, f32[1024,256]{1,0:T(8,128)}) custom-call(s32[1]{0:T(128)S(6)} %copy.12.len_ref, bf16[1,128,2048]{2,1,0:T(8,128)(2,1)} %x_ref.1, bf16[1,128,2048]{2,1,0:T(8,128)(2,1)} %q_ref.1, bf16[1,128,2048]{2,1,0:T(8,128)(2,1)} %og_ref.1, ...), custom_call_target="tpu_custom_call" | custom-call | tf_op jit(solution)/shard_map/pallas_call | solution.py:436
  66.0 2.9 %shard_map.112 = (bf16[1,128,2048]{2,1,0:T(8,128)(2,1)}, bf16[1,128,2048]{2,1,0:T(8,128)(2,1)}, f32[1024,256]{1,0:T(8,128)}, f32[1024,256]{1,0:T(8,128)}) custom-call(bf16[1,128,2048]{2,1,0:T(8,128)(2,1)} %get-tuple-element.8.refs_0_, bf16[1,128,2048]{2,1,0:T(8,128)(2,1)} %get-tuple-element.9.refs_1_, f32[1024,256]{1,0:T(8,128)} %get-tuple-element.10.refs_2_, ...), custom_call_target="tpu_custom_call" | custom-call | tf_op jit(solution)/shard_map/pallas_call | solution.py:464

commit v4 on v3

--- a/solution.py
+++ b/solution.py
@@ -61,7 +61,7 @@
     G, S, D,
     len_ref, x_ref, q_ref, og_ref, k_ref, v_ref, cos_ref, sin_ref,
     qg_ref, ig_ref, kw_ref, vw_ref,
-    wbuf, xbuf, xg, pgg, igs, igr, projected,
+    wbuf, xbuf, xg, pgg, igs, igr, projected, q_buf, og_buf, ld,
     zw_s, zw_r, xw_s, xw_r, yw_s, yw_r, ax_s, ax_r, by_s, by_r,
     xs_s, xs_r, zx_s, zx_r, xx_s, xx_r, cx_s, cx_r,
     zp_s, zp_r, xp_s, xp_r, ig_s, ig_r,
@@ -157,10 +157,16 @@
     repeat(1, S, lambda k: greet({"section": other_s(k)}))
     repeat(1, D, lambda k: greet({"dp": other_d(k)}))
     repeat(1, G, lambda k: greet({"groups": other_g(k)}))
-    wbuf[s, 0] = k_ref[...]
-    wbuf[s, 1] = v_ref[...]
-    for i in range(H):
-        xbuf[c * H + i] = x_ref[0, :, i * R : (i + 1) * R]
+    load = pltpu.make_async_copy
+    weights_in = [load(r, wbuf.at[s, i], ld.at[i]) for i, r in enumerate((k_ref, v_ref))]
+    inputs_here = [
+        load(x_ref.at[0, :, pl.ds(i * R, R)], xbuf.at[c * H + i], ld.at[2 + i]) for i in range(H)
+    ]
+    heads_in = [load(r, b, ld.at[2 + H + i]) for i, (r, b) in enumerate(((q_ref, q_buf), (og_ref, og_buf)))]
+    for copy in weights_in + inputs_here + heads_in:
+        copy.start()
+    for copy in weights_in:
+        copy.wait()
     pl.semaphore_wait(barrier, 1 + (S - 1) + (D - 1) + (G - 1))
 
     def along_line(k, body):
@@ -181,9 +187,11 @@
         def _():
             body(s - 1, 1)
 
-    x_sub(c).start()
     for half in range(CHUNKS):
         both_ways(lambda to, way: w_z(to, way, s, half).start())
+    for copy in inputs_here:
+        copy.wait()
+    x_sub(c).start()
     x_sub(1 - c).wait_recv()
     xg[s, d, my_tokens] = xbuf[s, my_tokens]
     repeat(1, D, lambda j: x_x(other_d(j), s, d).start())
@@ -254,6 +262,8 @@
     repeat(1, S, lambda k: along_line(k, project))
     repeat(1, S, inputs_on)
 
+    for copy in heads_in:
+        copy.wait()
     cos, sin = cos_ref[...], sin_ref[...]
     length = len_ref[0]
     u_ids = lax.broadcasted_iota(jnp.int32, (T, T), 0)
@@ -267,7 +277,7 @@
         value_grad = jnp.zeros((T, HEAD_SIZE), F32)
         for j in range(QUERY_GROUP):
             at = slice((h * QUERY_GROUP + j) * HEAD_SIZE, (h * QUERY_GROUP + j + 1) * HEAD_SIZE)
-            query, grad = q_ref[0, :, at], og_ref[0, :, at]
+            query, grad = q_buf[0, :, at], og_buf[0, :, at]
             scores = jnp.where(allowed, dot_nt(keys, query) * score_scale, -1e30)
             exponent = jnp.exp(scores - jnp.max(scores, axis=0, keepdims=True))
             probs = exponent / jnp.sum(exponent, axis=0, keepdims=True)
@@ -441,7 +451,7 @@
             jax.ShapeDtypeStruct((R, C), F32),
             jax.ShapeDtypeStruct((R, C), F32),
         ),
-        in_specs=[pl.BlockSpec(memory_space=pltpu.SMEM)] + [vmem] * 7,
+        in_specs=[pl.BlockSpec(memory_space=pltpu.SMEM)] + [pl.BlockSpec(memory_space=pl.ANY)] * 5 + [vmem] * 2,
         out_specs=(vmem,) * 4,
         scratch_shapes=[
             pltpu.VMEM((S, CHUNKS, R, C), BF16),
@@ -451,6 +461,9 @@
             pltpu.VMEM((H, T, R), F32),
             pltpu.VMEM((H, T, R), F32),
             pltpu.VMEM((T, 2 * C), F32),
+            pltpu.VMEM(queries.shape, BF16),
+            pltpu.VMEM(queries.shape, BF16),
+            dma((4 + H,)),
             dma((2, S, CHUNKS)), dma((S, CHUNKS)), *pairs(S, D, CHUNKS), *pairs(S, G, CHUNKS),
             *pairs(S, G, D, CHUNKS), *pairs(S, G, D, CHUNKS),
             *pairs(1), *pairs(S), *pairs(S, D), *pairs(1),

time: 69.1 us -> 68.3 us (0.988)
  Pallas kernels: 67.6 us -> 66.8 us
    pallas_call x1, Pallas kernels: 64.7 us -> 63.9 us  [shards(): pl.pallas_call(functools.partial(kernel, G, S, D), out_shape=(jax.ShapeDt...]
where the time goes in v4:
time: 68.3 us; the launch traced here: 68.1 us
  Pallas kernels  66.8 us (98%)
  between operations  1.29 us (2%)
    pallas_call x1, Pallas kernels, shards(): pl.pallas_call(functools.partial(kernel, G, S, D), out_shape=(jax.ShapeDt...  63.9 us
    pallas_call x1, Pallas kernels, shards(): pl.pallas_call(hand_out, out_shape=tuple((jax.ShapeDtypeStruct(r.shape, r...  2.93 us

profile of v4, /device:TPU:0, one launch (start us, length us, event | category | flops | bytes accessed | tf_op | source)
XLA Modules:
  0.0 68.1 jit_solution(8304657341319026085)
XLA Ops:
  1.3 63.9 %shard_map.111 = (bf16[1,128,2048]{2,1,0:T(8,128)(2,1)}, bf16[1,128,2048]{2,1,0:T(8,128)(2,1)}, f32[1024,256]{1,0:T(8,128)}, f32[1024,256]{1,0:T(8,128)}) custom-call(s32[1]{0:T(128)S(6)} %copy.12.len_ref, bf16[1,128,2048]{2,1,0:T(8,128)(2,1)} %x_ref.1, bf16[1,128,2048]{2,1,0:T(8,128)(2,1)} %q_ref.1, bf16[1,128,2048]{2,1,0:T(8,128)(2,1)} %og_ref.1, ...), custom_call_target="tpu_custom_call" | custom-call | tf_op jit(solution)/shard_map/pallas_call | solution.py:446
  65.2 2.9 %shard_map.112 = (bf16[1,128,2048]{2,1,0:T(8,128)(2,1)}, bf16[1,128,2048]{2,1,0:T(8,128)(2,1)}, f32[1024,256]{1,0:T(8,128)}, f32[1024,256]{1,0:T(8,128)}) custom-call(bf16[1,128,2048]{2,1,0:T(8,128)(2,1)} %get-tuple-element.8.refs_0_, bf16[1,128,2048]{2,1,0:T(8,128)(2,1)} %get-tuple-element.9.refs_1_, f32[1024,256]{1,0:T(8,128)} %get-tuple-element.10.refs_2_, ...), custom_call_target="tpu_custom_call" | custom-call | tf_op jit(solution)/shard_map/pallas_call | solution.py:477
